TPU v7x, 32 devices: a whole 2x2x4 slice. The times are simulated.
32 devices in a mesh: segment: 4 (over z), row: 4 (over y, x), dp: 2 (over core).
Axes of the slice: x: 2, y: 2, z: 4, core: 2. Of those that a mesh axis runs over, the one named last changes fastest.
Arguments:
- features: bfloat16 [4, 64, 64, 128], P('dp', 'row'), may hold values from -6 to 6
- residues: int32 [4], P('dp'), may hold values from 32 to 64, as said below
- blocks: int32 [4], P('segment'), may hold values from 1 to 3, as said below
- weights: bfloat16 [4, 3, 9, 128, 128], P('segment'), may hold values from -0.125 to 0.125
- cotangent: bfloat16 [4, 64, 64, 128], P('dp', 'row'), may hold values from -0.046875 to 0.046875
Outputs:
- weight_grads: float32 [4, 3, 9, 128, 128], P('segment')
Inputs may be any that keep to these rules, and one draw needn't show every extreme that they name: `residues`: rows of a complex at or beyond its residue count are padding. `blocks`: slots of a section at or beyond its count are skipped.
All inputs are finite; a program needn't handle non-finite values.
Results may differ from a plain program's by a relative error of at most 0.017.
Values may be sent and summed in bfloat16 or wider, within the bound.
A program may use at most 64 MiB of HBM per device.

v0:
```python
import jax
import jax.numpy as jnp
from jax import lax
from jax.sharding import PartitionSpec as P

HALO = 8


def padded_2(block, sides, width):
    for axis, dim in sides:
        count = lax.axis_size(axis)
        forward = [(i, i + 1) for i in range(count - 1)]
        backward = [(target, source) for source, target in forward]
        low = lax.ppermute(
            lax.slice_in_dim(block, block.shape[dim] - width, None, axis=dim), axis, forward
        )
        high = lax.ppermute(lax.slice_in_dim(block, 0, width, axis=dim), axis, backward)
        block = jnp.concatenate([low, block, high], axis=dim)
    return block


def passed_along(value, axis, steps):
    count = lax.axis_size(axis)
    leading, last = (max(0, -steps), min(count, count - steps))
    return lax.ppermute(value, axis, [(source, source + steps) for source in range(leading, last)])


def widen_columns(values):
    return jnp.pad(values, ((0, 0), (HALO, HALO), (0, 0)))


def elu_rounded(values):
    return jax.nn.elu(values.astype(jnp.float32)).astype(jnp.bfloat16)


def shifted_piece(padded, row_start, col_start, height, width):
    zero_start = jnp.zeros((), jnp.int32)
    return lax.dynamic_slice(
        padded, (row_start, col_start, zero_start), (height, width, padded.shape[2])
    )


def block_forward(padded, resident, weight_slot, dilation, keep_rows):
    height, width, channels = resident.shape
    total = jnp.zeros((height * width, channels), jnp.float32)
    for row_step in (-1, 0, 1):
        for col_step in (-1, 0, 1):
            tap_index = 3 * (row_step + 1) + col_step + 1
            piece = shifted_piece(
                padded, HALO + row_step * dilation, HALO + col_step * dilation, height, width
            )
            total = total + jnp.dot(
                piece.reshape(height * width, channels),
                weight_slot[tap_index],
                preferred_element_type=jnp.float32,
            )
    summed = resident.astype(jnp.float32) + total.reshape(height, width, channels)
    return (summed * keep_rows[:, None, None]).astype(jnp.bfloat16)


def block_backward(padded_act, padded_cot, masked_cot, resident, weight_slot, dilation):
    height, width, channels = masked_cot.shape
    flat_cot = masked_cot.reshape(height * width, channels)
    weight_terms = []
    back_sum = jnp.zeros((height * width, channels), jnp.float32)
    for row_step in (-1, 0, 1):
        for col_step in (-1, 0, 1):
            tap_index = 3 * (row_step + 1) + col_step + 1
            act_piece = shifted_piece(
                padded_act, HALO + row_step * dilation, HALO + col_step * dilation, height, width
            )
            weight_terms.append(
                jnp.einsum(
                    "pc,pd->cd",
                    act_piece.reshape(height * width, channels),
                    flat_cot,
                    preferred_element_type=jnp.float32,
                )
            )
            cot_piece = shifted_piece(
                padded_cot, HALO - row_step * dilation, HALO - col_step * dilation, height, width
            )
            back_sum = back_sum + jnp.einsum(
                "pd,cd->pc",
                cot_piece.reshape(height * width, channels),
                weight_slot[tap_index],
                preferred_element_type=jnp.float32,
            )
    resident_f = resident.astype(jnp.float32).reshape(height * width, channels)
    slope = jnp.where(resident_f > 0, 1.0, jnp.exp(jnp.minimum(resident_f, 0.0)))
    new_cot = (flat_cot.astype(jnp.float32) + slope * back_sum).astype(jnp.bfloat16)
    return (jnp.stack(weight_terms), new_cot.reshape(height, width, channels))


def store_slot(saved, slot_index, micro_clip, values, running):
    current = saved[slot_index, micro_clip]
    return saved.at[slot_index, micro_clip].set(jnp.where(running, values, current))


def body(features, residues, blocks, weights, cotangent):
    segment_count = lax.axis_size("segment")
    segment_index = lax.axis_index("segment")
    micro_count = features.shape[0]
    height, width, channels = (features.shape[1], features.shape[2], features.shape[3])
    slot_count = weights.shape[1]
    row_first = lax.axis_index("row") * height
    row_ids = row_first + jnp.arange(height, dtype=jnp.int32)
    active_blocks = blocks[0]
    weight_here = weights[0]
    dilations = [
        jnp.left_shift(jnp.int32(1), (slot_count * segment_index + slot_index) % 4)
        for slot_index in range(slot_count)
    ]
    tick_total = segment_count + micro_count - 1
    zero_value = jnp.zeros((), jnp.bfloat16)

    def forward_tick(tick_index, carry):
        incoming, saved_act, saved_res = carry
        micro = tick_index - segment_index
        running = (micro >= 0) & (micro < micro_count)
        micro_clip = jnp.clip(micro, 0, micro_count - 1)
        limit = residues[micro_clip]
        first_input = jnp.where((row_ids < limit)[:, None, None], features[micro_clip], zero_value)
        resident = jnp.where(segment_index == 0, first_input, incoming)
        keep_rows = (row_ids < limit).astype(jnp.float32)
        for slot_index in range(slot_count):
            active_here = running & (slot_index < active_blocks)
            activation = elu_rounded(resident)
            bordered = padded_2(activation, (("row", 0),), HALO)
            padded = widen_columns(bordered)
            saved_act = store_slot(saved_act, slot_index, micro_clip, padded, running)
            saved_res = store_slot(saved_res, slot_index, micro_clip, resident, running)
            resident = lax.cond(
                active_here,
                lambda packed: block_forward(
                    packed[0], packed[1], weight_here[slot_index], dilations[slot_index], keep_rows
                ),
                lambda packed: packed[1],
                (padded, resident),
            )
        outgoing = passed_along(resident, "segment", 1)
        return (outgoing, saved_act, saved_res)

    saved_act = jnp.zeros(
        (slot_count, micro_count, height + 2 * HALO, width + 2 * HALO, channels), jnp.bfloat16
    )
    saved_res = jnp.zeros((slot_count, micro_count, height, width, channels), jnp.bfloat16)
    start_carry = (jnp.zeros((height, width, channels), jnp.bfloat16), saved_act, saved_res)
    last_out, saved_act, saved_res = lax.fori_loop(0, tick_total, forward_tick, start_carry)

    def backward_tick(tick_index, carry):
        incoming, grads = carry
        micro = tick_index - (segment_count - 1 - segment_index)
        running = (micro >= 0) & (micro < micro_count)
        micro_clip = jnp.clip(micro, 0, micro_count - 1)
        keep_mask = (row_ids < residues[micro_clip])[:, None, None]
        grad_now = jnp.where(segment_index == segment_count - 1, cotangent[micro_clip], incoming)
        for slot_index in reversed(range(slot_count)):
            active_here = running & (slot_index < active_blocks)
            resident = saved_res[slot_index, micro_clip]
            masked_cot = jnp.where(keep_mask, grad_now, zero_value)
            padded_cot = widen_columns(padded_2(masked_cot, (("row", 0),), HALO))
            padded_act = saved_act[slot_index, micro_clip]
            weight_grad, grad_now = lax.cond(
                active_here,
                lambda packed: block_backward(
                    packed[0],
                    packed[1],
                    packed[2],
                    packed[3],
                    weight_here[slot_index],
                    dilations[slot_index],
                ),
                lambda packed: (jnp.zeros((9, channels, channels), jnp.float32), packed[4]),
                (padded_act, padded_cot, masked_cot, resident, grad_now),
            )
            grads = grads.at[slot_index].add(weight_grad)
        outgoing = passed_along(grad_now, "segment", -1)
        return (outgoing, grads)

    grad_start = (
        jnp.zeros((height, width, channels), jnp.bfloat16),
        jnp.zeros((slot_count, 9, channels, channels), jnp.float32),
    )
    last_cot, grads = lax.fori_loop(0, tick_total, backward_tick, grad_start)
    summed = lax.psum(grads.astype(jnp.bfloat16), ("row", "dp")).astype(jnp.float32)
    return summed[None]


def solution(mesh):
    in_specs = (
        P("dp", "row", None, None),
        P("dp"),
        P("segment"),
        P("segment", None, None, None, None),
        P("dp", "row", None, None),
    )
    out_specs = P("segment", None, None, None, None)
    return jax.shard_map(body, mesh=mesh, in_specs=in_specs, out_specs=out_specs, check_vma=False)
```

profile of v0, /device:TPU:0, one launch (start us, length us, event | category | flops | bytes accessed | tf_op | source)
XLA Modules:
  0.0 824.6 jit_solution(5124224164522853837)
XLA Ops:
  11.2 266.7 %while.48 = (s32[]{:T(128)}, bf16[16,64,128]{2,1,0:T(8,128)(2,1)S(1)}, bf16[3,2,32,80,128]{4,3,2,1,0:T(8,128)(2,1)}, bf16[3,2,16,64,128]{4,3,2,1,0:T(8,128)(2,1)...) while((s32[]{:T(128)}, ...), condition=%wide.region_10.11_spmd.clone, body=%wide.region_0.10_spmd.clone.sunk | while | flops 939262080 | bytes 78356784 | solution.py:149
  43.3 5.9 collective-permute-start.5
  91.6 5.9 collective-permute-start.5
  102.5 9.9 %collective-permute-start.6 = (bf16[16,64,128]{2,1,0:T(8,128)(2,1)S(1)}, bf16[16,64,128]{2,1,0:T(8,128)(2,1)S(1)}, u32[]{:S(2)}, u32[]{:S(2)}) collective-permute-start(bf16[16,64,128]{2,1,0:T(8,128)(2,1)S(1)} %get-tuple-element.1850), channel_id=1, source_target_pairs={{0,8},{8,16},{16,24},{1,9},{9,17},{17,25},{2,10},{10,18},{18,26},{... | collective-permute-start | bytes 786440 | tf_op jit(solution)/shard_map/while/body/eval_jaxpr/ppermute | solution.py:25
  145.6 5.9 collective-permute-start.5
  156.5 13.8 %collective-permute-start.6 = (bf16[16,64,128]{2,1,0:T(8,128)(2,1)S(1)}, bf16[16,64,128]{2,1,0:T(8,128)(2,1)S(1)}, u32[]{:S(2)}, u32[]{:S(2)}) collective-permute-start(bf16[16,64,128]{2,1,0:T(8,128)(2,1)S(1)} %get-tuple-element.1850), channel_id=1, source_target_pairs={{0,8},{8,16},{16,24},{1,9},{9,17},{17,25},{2,10},{10,18},{18,26},{... | collective-permute-start | bytes 786440 | tf_op jit(solution)/shard_map/while/body/eval_jaxpr/ppermute | solution.py:25
  203.5 5.9 collective-permute-start.5
  252.0 5.9 collective-permute-start.5
  262.9 11.1 %collective-permute-start.6 = (bf16[16,64,128]{2,1,0:T(8,128)(2,1)S(1)}, bf16[16,64,128]{2,1,0:T(8,128)(2,1)S(1)}, u32[]{:S(2)}, u32[]{:S(2)}) collective-permute-start(bf16[16,64,128]{2,1,0:T(8,128)(2,1)S(1)} %get-tuple-element.1850), channel_id=1, source_target_pairs={{0,8},{8,16},{16,24},{1,9},{9,17},{17,25},{2,10},{10,18},{18,26},{... | collective-permute-start | bytes 786440 | tf_op jit(solution)/shard_map/while/body/eval_jaxpr/ppermute | solution.py:25
  278.1 479.3 %while.49 = (s32[]{:T(128)}, bf16[16,64,128]{2,1,0:T(8,128)(2,1)S(1)}, f32[3,9,128,128]{3,2,1,0:T(8,128)S(1)}, s32[]{:T(128)}, pred[]{:T(512)}, /*index=5*/pred[...) while((s32[]{:T(128)}, ...), condition=%wide.region_18.19_spmd.clone, body=%wide.region_11.18_spmd.clone.sunk | while | flops 1820770304 | bytes 84773120 | solution.py:185
  282.5 6.1 collective-permute-start.8
  322.2 7.0 collective-permute-done.13
  333.4 5.9 collective-permute-start.8
  352.2 5.8 collective-permute-done.9
  372.8 6.0 collective-permute-done.13
  382.9 6.1 collective-permute-start.8
  422.7 151.7 %collective-permute-done.13 = bf16[16,64,128]{2,1,0:T(8,128)(2,1)S(1)} collective-permute-done((bf16[16,64,128]{2,1,0:T(8,128)(2,1)}, bf16[16,64,128]{2,1,0:T(8,128)(2,1)S(1)}, u32[]{:S(2)}, u32[]{:S(2)}) %collective-permute-start.13) | collective-permute-done | bytes 262176 | tf_op jit(solution)/shard_map/while/body/eval_jaxpr/ppermute | solution.py:25
  578.5 6.1 collective-permute-start.8
  614.4 21.7 %conditional.23 = (bf16[16,64,128]{2,1,0:T(8,128)(2,1)}, f32[1,9,128,128]{3,2,1,0:T(8,128)}) conditional(s32[]{:T(128)} %convert_element_type.333, bf16[16,64,128]{2,1,0:T(8,128)(2,1)} %get-tuple-element.1700, (bf16[16,64,128]{2,1,0:T(8,128)(2,1)S(1)}, bf16[3,2,16,64,128]{4,3,2,1,0:T(8,128)(2,1)}, s32[]{:T(128)}, ...), branch_computations={%region_16.16_spmd, %region_17.17_spmd} | conditional | flops 606076928 | bytes 22643180 | solution.py:164
  638.6 47.6 %collective-permute-done.13 = bf16[16,64,128]{2,1,0:T(8,128)(2,1)S(1)} collective-permute-done((bf16[16,64,128]{2,1,0:T(8,128)(2,1)}, bf16[16,64,128]{2,1,0:T(8,128)(2,1)S(1)}, u32[]{:S(2)}, u32[]{:S(2)}) %collective-permute-start.13) | collective-permute-done | bytes 262176 | tf_op jit(solution)/shard_map/while/body/eval_jaxpr/ppermute | solution.py:25
  690.4 7.1 collective-permute-start.8
  727.3 21.7 %conditional.23 = (bf16[16,64,128]{2,1,0:T(8,128)(2,1)}, f32[1,9,128,128]{3,2,1,0:T(8,128)}) conditional(s32[]{:T(128)} %convert_element_type.333, bf16[16,64,128]{2,1,0:T(8,128)(2,1)} %get-tuple-element.1700, (bf16[16,64,128]{2,1,0:T(8,128)(2,1)S(1)}, bf16[3,2,16,64,128]{4,3,2,1,0:T(8,128)(2,1)}, s32[]{:T(128)}, ...), branch_computations={%region_16.16_spmd, %region_17.17_spmd} | conditional | flops 606076928 | bytes 22643180 | solution.py:164
  751.5 6.0 collective-permute-done.13
  758.5 56.6 %all-reduce.8.cloned.1.call-done = bf16[1,3,9,128,128]{4,3,2,1,0:T(8,128)(2,1)} async-done(((bf16[1,3,9,128,128]{4,3,2,1,0:T(8,128)(2,1)}), bf16[1,3,9,128,128]{4,3,2,1,0:T(8,128)(2,1)}) %all-reduce.8.cloned.1.call-update) | async-done | bytes 884752 | tf_op jit(solution)/shard_map/psum | solution.py:186
  (486 shorter events, 448.9 us)
Async XLA Ops:
  6.5 808.6 %all-reduce.8.cloned.1.call-start = ((), (), s32[]{:S(2)}) async-start(), calls=%async_computation | async-start | bytes 1769472 | tf_op jit(solution)/shard_map/psum | solution.py:186
  29.9 11.7 %collective-permute-start.2 = (bf16[8,64,128]{2,1,0:T(8,128)(2,1)S(1)}, bf16[8,64,128]{2,1,0:T(8,128)(2,1)S(1)}, u32[]{:S(2)}, u32[]{:S(2)}) collective-permute-start(bf16[8,64,128]{2,1,0:T(8,128)(2,1)S(1)} %get-tuple-element.1669), channel_id=1, source_target_pairs={{2,0},{4,2},{6,4},{3,1},{5,3},{7,5},{10,8},{12,10},{14,12},{11,9},... | collective-permute-start | bytes 393224 | tf_op jit(solution)/shard_map/while/body/eval_jaxpr/ppermute | solution.py:17
  31.2 10.4 %collective-permute-start.3 = (bf16[8,64,128]{2,1,0:T(8,128)(2,1)S(1)}, bf16[8,64,128]{2,1,0:T(8,128)(2,1)S(1)}, u32[]{:S(2)}, u32[]{:S(2)}) collective-permute-start(bf16[8,64,128]{2,1,0:T(8,128)(2,1)S(1)} %get-tuple-element.1670), channel_id=1, source_target_pairs={{0,2},{2,4},{4,6},{1,3},{3,5},{5,7},{8,10},{10,12},{12,14},{9,11},... | collective-permute-start | bytes 393224 | tf_op jit(solution)/shard_map/while/body/eval_jaxpr/ppermute | solution.py:14
  42.0 11.5 %collective-permute-start.4 = (bf16[8,64,128]{2,1,0:T(8,128)(2,1)S(1)}, bf16[8,64,128]{2,1,0:T(8,128)(2,1)S(1)}, u32[]{:S(2)}, u32[]{:S(2)}) collective-permute-start(bf16[8,64,128]{2,1,0:T(8,128)(2,1)S(1)} %get-tuple-element.1671), channel_id=1, source_target_pairs={{2,0},{4,2},{6,4},{3,1},{5,3},{7,5},{10,8},{12,10},{14,12},{11,9},... | collective-permute-start | bytes 393224 | tf_op jit(solution)/shard_map/while/body/eval_jaxpr/ppermute | solution.py:17
  77.9 12.0 %collective-permute-start.2 = (bf16[8,64,128]{2,1,0:T(8,128)(2,1)S(1)}, bf16[8,64,128]{2,1,0:T(8,128)(2,1)S(1)}, u32[]{:S(2)}, u32[]{:S(2)}) collective-permute-start(bf16[8,64,128]{2,1,0:T(8,128)(2,1)S(1)} %get-tuple-element.1669), channel_id=1, source_target_pairs={{2,0},{4,2},{6,4},{3,1},{5,3},{7,5},{10,8},{12,10},{14,12},{11,9},... | collective-permute-start | bytes 393224 | tf_op jit(solution)/shard_map/while/body/eval_jaxpr/ppermute | solution.py:17
  79.2 10.7 %collective-permute-start.3 = (bf16[8,64,128]{2,1,0:T(8,128)(2,1)S(1)}, bf16[8,64,128]{2,1,0:T(8,128)(2,1)S(1)}, u32[]{:S(2)}, u32[]{:S(2)}) collective-permute-start(bf16[8,64,128]{2,1,0:T(8,128)(2,1)S(1)} %get-tuple-element.1670), channel_id=1, source_target_pairs={{0,2},{2,4},{4,6},{1,3},{3,5},{5,7},{8,10},{10,12},{12,14},{9,11},... | collective-permute-start | bytes 393224 | tf_op jit(solution)/shard_map/while/body/eval_jaxpr/ppermute | solution.py:14
  90.3 11.5 %collective-permute-start.4 = (bf16[8,64,128]{2,1,0:T(8,128)(2,1)S(1)}, bf16[8,64,128]{2,1,0:T(8,128)(2,1)S(1)}, u32[]{:S(2)}, u32[]{:S(2)}) collective-permute-start(bf16[8,64,128]{2,1,0:T(8,128)(2,1)S(1)} %get-tuple-element.1671), channel_id=1, source_target_pairs={{2,0},{4,2},{6,4},{3,1},{5,3},{7,5},{10,8},{12,10},{14,12},{11,9},... | collective-permute-start | bytes 393224 | tf_op jit(solution)/shard_map/while/body/eval_jaxpr/ppermute | solution.py:17
  91.6 10.2 %collective-permute-start.5 = (bf16[8,64,128]{2,1,0:T(8,128)(2,1)S(1)}, bf16[8,64,128]{2,1,0:T(8,128)(2,1)S(1)}, u32[]{:S(2)}, u32[]{:S(2)}) collective-permute-start(bf16[8,64,128]{2,1,0:T(8,128)(2,1)S(1)} %get-tuple-element.1672), channel_id=1, source_target_pairs={{0,2},{2,4},{4,6},{1,3},{3,5},{5,7},{8,10},{10,12},{12,14},{9,11},... | collective-permute-start | bytes 393224 | tf_op jit(solution)/shard_map/while/body/eval_jaxpr/ppermute | solution.py:14
  102.5 13.7 %collective-permute-start.6 = (bf16[16,64,128]{2,1,0:T(8,128)(2,1)S(1)}, bf16[16,64,128]{2,1,0:T(8,128)(2,1)S(1)}, u32[]{:S(2)}, u32[]{:S(2)}) collective-permute-start(bf16[16,64,128]{2,1,0:T(8,128)(2,1)S(1)} %get-tuple-element.1850), channel_id=1, source_target_pairs={{0,8},{8,16},{16,24},{1,9},{9,17},{17,25},{2,10},{10,18},{18,26},{... | collective-permute-start | bytes 786440 | tf_op jit(solution)/shard_map/while/body/eval_jaxpr/ppermute | solution.py:25
  131.9 12.0 %collective-permute-start.2 = (bf16[8,64,128]{2,1,0:T(8,128)(2,1)S(1)}, bf16[8,64,128]{2,1,0:T(8,128)(2,1)S(1)}, u32[]{:S(2)}, u32[]{:S(2)}) collective-permute-start(bf16[8,64,128]{2,1,0:T(8,128)(2,1)S(1)} %get-tuple-element.1669), channel_id=1, source_target_pairs={{2,0},{4,2},{6,4},{3,1},{5,3},{7,5},{10,8},{12,10},{14,12},{11,9},... | collective-permute-start | bytes 393224 | tf_op jit(solution)/shard_map/while/body/eval_jaxpr/ppermute | solution.py:17
  133.2 10.7 %collective-permute-start.3 = (bf16[8,64,128]{2,1,0:T(8,128)(2,1)S(1)}, bf16[8,64,128]{2,1,0:T(8,128)(2,1)S(1)}, u32[]{:S(2)}, u32[]{:S(2)}) collective-permute-start(bf16[8,64,128]{2,1,0:T(8,128)(2,1)S(1)} %get-tuple-element.1670), channel_id=1, source_target_pairs={{0,2},{2,4},{4,6},{1,3},{3,5},{5,7},{8,10},{10,12},{12,14},{9,11},... | collective-permute-start | bytes 393224 | tf_op jit(solution)/shard_map/while/body/eval_jaxpr/ppermute | solution.py:14
  144.3 11.5 %collective-permute-start.4 = (bf16[8,64,128]{2,1,0:T(8,128)(2,1)S(1)}, bf16[8,64,128]{2,1,0:T(8,128)(2,1)S(1)}, u32[]{:S(2)}, u32[]{:S(2)}) collective-permute-start(bf16[8,64,128]{2,1,0:T(8,128)(2,1)S(1)} %get-tuple-element.1671), channel_id=1, source_target_pairs={{2,0},{4,2},{6,4},{3,1},{5,3},{7,5},{10,8},{12,10},{14,12},{11,9},... | collective-permute-start | bytes 393224 | tf_op jit(solution)/shard_map/while/body/eval_jaxpr/ppermute | solution.py:17
  145.6 10.2 %collective-permute-start.5 = (bf16[8,64,128]{2,1,0:T(8,128)(2,1)S(1)}, bf16[8,64,128]{2,1,0:T(8,128)(2,1)S(1)}, u32[]{:S(2)}, u32[]{:S(2)}) collective-permute-start(bf16[8,64,128]{2,1,0:T(8,128)(2,1)S(1)} %get-tuple-element.1672), channel_id=1, source_target_pairs={{0,2},{2,4},{4,6},{1,3},{3,5},{5,7},{8,10},{10,12},{12,14},{9,11},... | collective-permute-start | bytes 393224 | tf_op jit(solution)/shard_map/while/body/eval_jaxpr/ppermute | solution.py:14
  156.5 17.7 %collective-permute-start.6 = (bf16[16,64,128]{2,1,0:T(8,128)(2,1)S(1)}, bf16[16,64,128]{2,1,0:T(8,128)(2,1)S(1)}, u32[]{:S(2)}, u32[]{:S(2)}) collective-permute-start(bf16[16,64,128]{2,1,0:T(8,128)(2,1)S(1)} %get-tuple-element.1850), channel_id=1, source_target_pairs={{0,8},{8,16},{16,24},{1,9},{9,17},{17,25},{2,10},{10,18},{18,26},{... | collective-permute-start | bytes 786440 | tf_op jit(solution)/shard_map/while/body/eval_jaxpr/ppermute | solution.py:25
  189.8 12.0 %collective-permute-start.2 = (bf16[8,64,128]{2,1,0:T(8,128)(2,1)S(1)}, bf16[8,64,128]{2,1,0:T(8,128)(2,1)S(1)}, u32[]{:S(2)}, u32[]{:S(2)}) collective-permute-start(bf16[8,64,128]{2,1,0:T(8,128)(2,1)S(1)} %get-tuple-element.1669), channel_id=1, source_target_pairs={{2,0},{4,2},{6,4},{3,1},{5,3},{7,5},{10,8},{12,10},{14,12},{11,9},... | collective-permute-start | bytes 393224 | tf_op jit(solution)/shard_map/while/body/eval_jaxpr/ppermute | solution.py:17
  191.1 10.7 %collective-permute-start.3 = (bf16[8,64,128]{2,1,0:T(8,128)(2,1)S(1)}, bf16[8,64,128]{2,1,0:T(8,128)(2,1)S(1)}, u32[]{:S(2)}, u32[]{:S(2)}) collective-permute-start(bf16[8,64,128]{2,1,0:T(8,128)(2,1)S(1)} %get-tuple-element.1670), channel_id=1, source_target_pairs={{0,2},{2,4},{4,6},{1,3},{3,5},{5,7},{8,10},{10,12},{12,14},{9,11},... | collective-permute-start | bytes 393224 | tf_op jit(solution)/shard_map/while/body/eval_jaxpr/ppermute | solution.py:14
  202.2 11.5 %collective-permute-start.4 = (bf16[8,64,128]{2,1,0:T(8,128)(2,1)S(1)}, bf16[8,64,128]{2,1,0:T(8,128)(2,1)S(1)}, u32[]{:S(2)}, u32[]{:S(2)}) collective-permute-start(bf16[8,64,128]{2,1,0:T(8,128)(2,1)S(1)} %get-tuple-element.1671), channel_id=1, source_target_pairs={{2,0},{4,2},{6,4},{3,1},{5,3},{7,5},{10,8},{12,10},{14,12},{11,9},... | collective-permute-start | bytes 393224 | tf_op jit(solution)/shard_map/while/body/eval_jaxpr/ppermute | solution.py:17
  203.5 10.2 %collective-permute-start.5 = (bf16[8,64,128]{2,1,0:T(8,128)(2,1)S(1)}, bf16[8,64,128]{2,1,0:T(8,128)(2,1)S(1)}, u32[]{:S(2)}, u32[]{:S(2)}) collective-permute-start(bf16[8,64,128]{2,1,0:T(8,128)(2,1)S(1)} %get-tuple-element.1672), channel_id=1, source_target_pairs={{0,2},{2,4},{4,6},{1,3},{3,5},{5,7},{8,10},{10,12},{12,14},{9,11},... | collective-permute-start | bytes 393224 | tf_op jit(solution)/shard_map/while/body/eval_jaxpr/ppermute | solution.py:14
  238.4 12.0 %collective-permute-start.2 = (bf16[8,64,128]{2,1,0:T(8,128)(2,1)S(1)}, bf16[8,64,128]{2,1,0:T(8,128)(2,1)S(1)}, u32[]{:S(2)}, u32[]{:S(2)}) collective-permute-start(bf16[8,64,128]{2,1,0:T(8,128)(2,1)S(1)} %get-tuple-element.1669), channel_id=1, source_target_pairs={{2,0},{4,2},{6,4},{3,1},{5,3},{7,5},{10,8},{12,10},{14,12},{11,9},... | collective-permute-start | bytes 393224 | tf_op jit(solution)/shard_map/while/body/eval_jaxpr/ppermute | solution.py:17
  239.7 10.7 %collective-permute-start.3 = (bf16[8,64,128]{2,1,0:T(8,128)(2,1)S(1)}, bf16[8,64,128]{2,1,0:T(8,128)(2,1)S(1)}, u32[]{:S(2)}, u32[]{:S(2)}) collective-permute-start(bf16[8,64,128]{2,1,0:T(8,128)(2,1)S(1)} %get-tuple-element.1670), channel_id=1, source_target_pairs={{0,2},{2,4},{4,6},{1,3},{3,5},{5,7},{8,10},{10,12},{12,14},{9,11},... | collective-permute-start | bytes 393224 | tf_op jit(solution)/shard_map/while/body/eval_jaxpr/ppermute | solution.py:14
  250.7 11.5 %collective-permute-start.4 = (bf16[8,64,128]{2,1,0:T(8,128)(2,1)S(1)}, bf16[8,64,128]{2,1,0:T(8,128)(2,1)S(1)}, u32[]{:S(2)}, u32[]{:S(2)}) collective-permute-start(bf16[8,64,128]{2,1,0:T(8,128)(2,1)S(1)} %get-tuple-element.1671), channel_id=1, source_target_pairs={{2,0},{4,2},{6,4},{3,1},{5,3},{7,5},{10,8},{12,10},{14,12},{11,9},... | collective-permute-start | bytes 393224 | tf_op jit(solution)/shard_map/while/body/eval_jaxpr/ppermute | solution.py:17
  262.9 14.9 %collective-permute-start.6 = (bf16[16,64,128]{2,1,0:T(8,128)(2,1)S(1)}, bf16[16,64,128]{2,1,0:T(8,128)(2,1)S(1)}, u32[]{:S(2)}, u32[]{:S(2)}) collective-permute-start(bf16[16,64,128]{2,1,0:T(8,128)(2,1)S(1)} %get-tuple-element.1850), channel_id=1, source_target_pairs={{0,8},{8,16},{16,24},{1,9},{9,17},{17,25},{2,10},{10,18},{18,26},{... | collective-permute-start | bytes 786440 | tf_op jit(solution)/shard_map/while/body/eval_jaxpr/ppermute | solution.py:25
  420.2 154.2 %collective-permute-start.13 = (bf16[16,64,128]{2,1,0:T(8,128)(2,1)}, bf16[16,64,128]{2,1,0:T(8,128)(2,1)S(1)}, u32[]{:S(2)}, u32[]{:S(2)}) collective-permute-start(bf16[16,64,128]{2,1,0:T(8,128)(2,1)} %get-tuple-element.1703), channel_id=1, source_target_pairs={{8,0},{16,8},{24,16},{9,1},{17,9},{25,17},{10,2},{18,10},{26,18},{... | collective-permute-start | bytes 786440 | tf_op jit(solution)/shard_map/while/body/eval_jaxpr/ppermute | solution.py:25
  636.1 50.1 %collective-permute-start.13 = (bf16[16,64,128]{2,1,0:T(8,128)(2,1)}, bf16[16,64,128]{2,1,0:T(8,128)(2,1)S(1)}, u32[]{:S(2)}, u32[]{:S(2)}) collective-permute-start(bf16[16,64,128]{2,1,0:T(8,128)(2,1)} %get-tuple-element.1703), channel_id=1, source_target_pairs={{8,0},{16,8},{24,16},{9,1},{17,9},{25,17},{10,2},{18,10},{26,18},{... | collective-permute-start | bytes 786440 | tf_op jit(solution)/shard_map/while/body/eval_jaxpr/ppermute | solution.py:25
  (70 other events, 445.5 us)
Sparse Core Ops, SparseCore 0:
  758.6 56.4 all-reduce.7
where the time goes:
time: 831 us; the launch traced here: 825 us
  waiting for transfers between devices  326 us (39%)
  starting transfers between devices  254 us (31%)
  other arithmetic  120 us (14%)
  local copies, waits for them, and re-layouts  67 us (8%)
  matrix products  40.8 us (5%)
  between operations  14.1 us (2%)
    ppermute x10, waiting for transfers between devices, passed_along(): lax.ppermute(value, axis, [(source, source + steps) for source in range(l...  224 us
    ppermute x30, starting transfers between devices, padded_2(): lax.ppermute(lax.slice_in_dim(block, block.shape[dim] - width, None, axis...  168 us
    scatter x30, other arithmetic, store_slot(): saved.at[slot_index, micro_clip].set(jnp.where(running, values, current))  57.1 us
    psum x1, waiting for transfers between devices, body(): lax.psum(grads.astype(jnp.bfloat16), ('row', 'dp')).astype(jnp.float32)  56.6 us
    ppermute x10, starting transfers between devices, passed_along(): lax.ppermute(value, axis, [(source, source + steps) for source in range(l...  47.1 us
    ppermute x30, starting transfers between devices, padded_2(): lax.ppermute(lax.slice_in_dim(block, 0, width, axis=dim), axis, backward)  38.8 us
    ppermute x30, waiting for transfers between devices, padded_2(): lax.ppermute(lax.slice_in_dim(block, 0, width, axis=dim), axis, backward)  34.1 us
    dynamic_slice x30, local copies, waits for them, and re-layouts, store_slot(): current = saved[slot_index, micro_clip]  31.6 us
  transfers between devices with their start and end apart: 71, of which 38 were waited for; matrix products, arithmetic and copies ran while one was open for 11% of the time, Pallas kernels for 0%

commit v1 on v0

--- a/solution.py
+++ b/solution.py
@@ -1,6 +1,10 @@
+import functools
+
 import jax
 import jax.numpy as jnp
 from jax import lax
+from jax.experimental import pallas as pl
+from jax.experimental.pallas import tpu as pltpu
 from jax.sharding import PartitionSpec as P
 
 HALO = 8
@@ -97,7 +101,7 @@
     return saved.at[slot_index, micro_clip].set(jnp.where(running, values, current))
 
 
-def body(features, residues, blocks, weights, cotangent):
+def relay_body(features, residues, blocks, weights, cotangent):
     segment_count = lax.axis_size("segment")
     segment_index = lax.axis_index("segment")
     micro_count = features.shape[0]
@@ -187,6 +191,187 @@
     return summed[None]
 
 
+VMEM_BUDGET = 44 * 2**20
+CHUNK = 8
+
+
+def chain_kernel(
+    slots, parts, segments,
+    info, blocks, features, cotangent, weights, weights_t, grads,
+    saved, wide, grad_now, sums,
+):
+    rows, width, channels = features.shape
+    rc = CHUNK
+    cells = rc * width
+    limit, own_segment, part = info[0], info[1], info[2]
+    total = segments * slots
+    own_rows = rows // parts
+    column = lax.broadcasted_iota(jnp.int32, (rc, width, channels), 1).reshape(cells, channels)
+    cell = lax.broadcasted_iota(jnp.int32, (cells, channels), 0)
+    before = []
+    count = jnp.int32(0)
+    for section in range(segments):
+        for slot in range(slots):
+            before.append(count + jnp.minimum(slot, blocks[section]))
+        count = count + blocks[section]
+
+    def widened(values, dilation, first, sign):
+        ahead = pltpu.roll(values, cells - dilation, 0)
+        ahead = jnp.where(column < width - dilation, ahead, 0.0)
+        behind = pltpu.roll(values, dilation, 0)
+        behind = jnp.where(column >= dilation, behind, 0.0)
+        left, right = (behind, ahead) if sign > 0 else (ahead, behind)
+        at = pl.ds(HALO + first, rc)
+        shape = (rc, width, channels)
+        wide[at, :, 0:channels] = left.astype(jnp.bfloat16).reshape(shape)
+        wide[at, :, channels:2 * channels] = values.astype(jnp.bfloat16).reshape(shape)
+        wide[at, :, 2 * channels:] = right.astype(jnp.bfloat16).reshape(shape)
+
+    def conv(taps, index, dilation, first, sign):
+        out = None
+        for row_step in (-1, 0, 1):
+            piece = wide[pl.ds(HALO + first + sign * row_step * dilation, rc)]
+            term = jnp.dot(
+                piece.reshape(cells, 3 * channels),
+                taps[index, row_step + 1],
+                preferred_element_type=jnp.float32,
+            )
+            out = term if out is None else out + term
+        return out
+
+    wide[0:HALO] = jnp.zeros((HALO, width, 3 * channels), jnp.bfloat16)
+    wide[HALO + rows:] = jnp.zeros((HALO, width, 3 * channels), jnp.bfloat16)
+    grads[...] = jnp.zeros_like(grads)
+
+    @pl.loop(0, rows // rc)
+    def _(i):
+        first = i * rc
+        values = features[pl.ds(first, rc)].reshape(cells, channels).astype(jnp.float32)
+        values = jnp.where(cell < (limit - first) * width, values, 0.0)
+        saved[0, pl.ds(first, rc)] = values.astype(jnp.bfloat16).reshape(rc, width, channels)
+
+    for index in range(total - 1):
+        section, slot = divmod(index, slots)
+        dilation = 2 ** (index % 4)
+        source = before[index]
+
+        @pl.when((slot < blocks[section]) & (source < count - 1))
+        def _():
+            @pl.loop(0, rows // rc)
+            def _(i):
+                first = i * rc
+                x = saved[source, pl.ds(first, rc)].reshape(cells, channels).astype(jnp.float32)
+                act = jnp.where(x > 0, x, jnp.exp(jnp.minimum(x, 0.0)) - 1.0)
+                widened(act, dilation, first, 1)
+
+            @pl.loop(0, rows // rc)
+            def _(i):
+                first = i * rc
+                out = conv(weights, index, dilation, first, 1)
+                x = saved[source, pl.ds(first, rc)].reshape(cells, channels).astype(jnp.float32)
+                x = jnp.where(cell < (limit - first) * width, x + out, 0.0)
+                saved[source + 1, pl.ds(first, rc)] = x.astype(jnp.bfloat16).reshape(rc, width, channels)
+
+    grad_now[...] = cotangent[...]
+
+    for index in reversed(range(total)):
+        section, slot = divmod(index, slots)
+        dilation = 2 ** (index % 4)
+        source = before[index]
+        active = (slot < blocks[section]) & (section >= own_segment)
+
+        @pl.when(active)
+        def _():
+            @pl.loop(0, rows // rc)
+            def _(i):
+                first = i * rc
+                g = grad_now[pl.ds(first, rc)].reshape(cells, channels).astype(jnp.float32)
+                g = jnp.where(cell < (limit - first) * width, g, 0.0)
+                widened(g, dilation, first, -1 * -1)
+
+        @pl.when(active & (section == own_segment))
+        def _():
+            sums[...] = jnp.zeros_like(sums)
+
+            @pl.loop(0, own_rows // rc)
+            def _(i):
+                first = part * own_rows + i * rc
+                x = saved[source, pl.ds(first, rc)].reshape(cells, channels).astype(jnp.float32)
+                act = jnp.where(x > 0, x, jnp.exp(jnp.minimum(x, 0.0)) - 1.0).astype(jnp.bfloat16)
+                for row_step in (-1, 0, 1):
+                    piece = wide[pl.ds(HALO + first - row_step * dilation, rc)]
+                    sums[row_step + 1] += lax.dot_general(
+                        act, piece.reshape(cells, 3 * channels),
+                        (((0,), (0,)), ((), ())),
+                        preferred_element_type=jnp.float32,
+                    )
+
+            for row_tap in range(3):
+                for col_tap in range(3):
+                    grads[slot, 3 * row_tap + col_tap] = sums[
+                        row_tap, :, (2 - col_tap) * channels:(3 - col_tap) * channels
+                    ].astype(jnp.bfloat16)
+
+        @pl.when(active & ((section > own_segment) | (slot > 0)))
+        def _():
+            @pl.loop(0, rows // rc)
+            def _(i):
+                first = i * rc
+                out = conv(weights_t, index, dilation, first, -1)
+                x = saved[source, pl.ds(first, rc)].reshape(cells, channels).astype(jnp.float32)
+                slope = jnp.where(x > 0, 1.0, jnp.exp(jnp.minimum(x, 0.0)))
+                masked = wide[pl.ds(HALO + first, rc), :, channels:2 * channels]
+                g = masked.reshape(cells, channels).astype(jnp.float32) + slope * out
+                grad_now[pl.ds(first, rc)] = g.astype(jnp.bfloat16).reshape(rc, width, channels)
+
+
+def whole_map_body(features, residues, blocks, weights, cotangent):
+    micro_count, height, width, channels = features.shape
+    slots = weights.shape[1]
+    segments = lax.axis_size("segment")
+    row_count = lax.axis_size("row")
+    parts = row_count // micro_count
+    rows = height * row_count
+    row_index = lax.axis_index("row")
+    micro = row_index // parts
+    info = jnp.stack([residues[micro], lax.axis_index("segment"), row_index % parts])
+    all_blocks = lax.all_gather(blocks, "segment", tiled=True)
+    taps = lax.all_gather(weights, "segment", tiled=True)
+    own = lax.all_gather(features, "row", axis=1, tiled=True)[micro]
+    own_cot = lax.all_gather(cotangent, "row", axis=1, tiled=True)[micro]
+    flat = taps.reshape(segments * slots, 3, 3, channels, channels)
+    straight = flat.reshape(segments * slots, 3, 3 * channels, channels)
+    turned = jnp.swapaxes(flat[:, :, ::-1], -1, -2).reshape(segments * slots, 3, 3 * channels, channels)
+    smem = pl.BlockSpec(memory_space=pltpu.SMEM)
+    vmem = pl.BlockSpec(memory_space=pltpu.VMEM)
+    grads = pl.pallas_call(
+        functools.partial(chain_kernel, slots, parts, segments),
+        out_shape=jax.ShapeDtypeStruct((slots, 9, channels, channels), jnp.bfloat16),
+        in_specs=[smem, smem, vmem, vmem, vmem, vmem],
+        out_specs=vmem,
+        scratch_shapes=[
+            pltpu.VMEM((segments * slots, rows, width, channels), jnp.bfloat16),
+            pltpu.VMEM((rows + 2 * HALO, width, 3 * channels), jnp.bfloat16),
+            pltpu.VMEM((rows, width, channels), jnp.bfloat16),
+            pltpu.VMEM((3, channels, 3 * channels), jnp.float32),
+        ],
+        compiler_params=pltpu.CompilerParams(vmem_limit_bytes=VMEM_BUDGET),
+        name="chain",
+    )(info, all_blocks, own, own_cot, straight, turned)
+    return lax.psum(grads, ("row", "dp")).astype(jnp.float32)[None]
+
+
+def body(features, residues, blocks, weights, cotangent):
+    micro_count, height, width, channels = features.shape
+    row_count, segments = lax.axis_size("row"), lax.axis_size("segment")
+    one_map = height * row_count * width * channels * 2
+    need = one_map * (weights.shape[1] * segments + 9) + 6 * segments * weights.size
+    fits = need < VMEM_BUDGET and row_count % micro_count == 0
+    fits = fits and (height * micro_count) % CHUNK == 0
+    run = whole_map_body if fits else relay_body
+    return run(features, residues, blocks, weights, cotangent)
+
+
 def solution(mesh):
     in_specs = (
         P("dp", "row", None, None),

time: 831 us -> 310 us (0.37)
  starting transfers between devices: 254 us -> 0.12 us
  waiting for transfers between devices: 326 us -> 185 us
  other arithmetic: 120 us -> 3.29 us
  Pallas kernels: 0 us -> 76.3 us
  local copies, waits for them, and re-layouts: 67 us -> 23.6 us
  matrix products: 40.8 us -> 0 us
  blocking collectives: 0 us -> 9.89 us
    ppermute x70 -> x0, waiting for transfers between devices: 270 us -> none  [the longest x10 224 us: passed_along(): lax.ppermute(value, axis, [(source, source + steps) for source in range(l...]
    ppermute x70 -> x0, starting transfers between devices: 254 us -> none  [the longest x30 168 us: padded_2(): lax.ppermute(lax.slice_in_dim(block, block.shape[dim] - width, None, axis...]
    all_gather x0 -> x3, waiting for transfers between devices: none -> 128 us  [the longest x1 69.3 us: whole_map_body(): taps = lax.all_gather(weights, 'segment', tiled=True)]
    pallas_call x0 -> x1, Pallas kernels: none -> 76.3 us  [whole_map_body(): pl.pallas_call(functools.partial(chain_kernel, slots, parts, segments), o...]
    scatter x30 -> x0, other arithmetic: 57.1 us -> none  [store_slot(): saved.at[slot_index, micro_clip].set(jnp.where(running, values, current))]
    dot_general x54 -> x0, matrix products: 40.8 us -> none  [the longest x18 31.5 us: block_backward(): jnp.einsum('pc,pd->cd', act_piece.reshape(height * width, channels), flat...]
    dynamic_slice x44 -> x1, local copies, waits for them, and re-layouts: 40.7 us -> 1.26 us  [whole_map_body(): residues[micro]]
    select_n x17 -> x0, other arithmetic: 21 us -> none  [the longest x15 18.8 us: backward_tick(): masked_cot = jnp.where(keep_mask, grad_now, zero_value)]
  transfers between devices with their start and end apart: 71 -> 4, of which waited for: 38 -> 4; matrix products, arithmetic and copies ran while one was open for 11% -> 3% of each run, Pallas kernels for 0% -> 0%
where the time goes in v1:
time: 310 us; the launch traced here: 311 us
  waiting for transfers between devices  185 us (60%)
  Pallas kernels  76.3 us (25%)
  local copies, waits for them, and re-layouts  23.6 us (8%)
  between operations  13.8 us (4%)
  blocking collectives  9.89 us (3%)
  other arithmetic  3.29 us (1%)
    pallas_call x1, Pallas kernels, whole_map_body(): pl.pallas_call(functools.partial(chain_kernel, slots, parts, segments), o...  76.3 us
    all_gather x1, waiting for transfers between devices, whole_map_body(): taps = lax.all_gather(weights, 'segment', tiled=True)  69.3 us
    psum x1, waiting for transfers between devices, whole_map_body(): return lax.psum(grads, ('row', 'dp')).astype(jnp.float32)[None]  54.2 us
    all_gather x1, waiting for transfers between devices, whole_map_body(): own_cot = lax.all_gather(cotangent, 'row', axis=1, tiled=True)[micro]  34.9 us
    all_gather x1, waiting for transfers between devices, whole_map_body(): own = lax.all_gather(features, 'row', axis=1, tiled=True)[micro]  24 us
    unnamed x1, blocking collectives  9.89 us
    unnamed x13, local copies, waits for them, and re-layouts  7.36 us
  transfers between devices with their start and end apart: 4, of which 4 were waited for; matrix products, arithmetic and copies ran while one was open for 3% of the time, Pallas kernels for 0%

profile of v1, /device:TPU:0, one launch (start us, length us, event | category | flops | bytes accessed | tf_op | source)
XLA Modules:
  0.0 311.5 jit_solution(11426178087481857755)
XLA Ops:
  6.5 0.7 all-gather.4.cloned.1.call-update
  7.3 0.0 all-gather.6.cloned.1.call-start
  7.3 0.7 all-gather.6.cloned.1.call-update
  8.1 0.7 all-gather.8.cloned.1.call-update
  8.7 0.0 all-reduce.3.cloned.1.call-start
  9.4 1.2 dynamic-slice
  10.7 0.8 dynamic-update-slice
  11.4 9.9 %all-reduce.blocks = s32[4]{0:T(128)S(1)} all-reduce(s32[4]{0:T(128)S(1)} %dynamic-update-slice), channel_id=1, replica_groups=mesh['segment'=4,'row'=4,'dp'=2] {'segment'}, use_global_device_ids=true, to_apply=%add | all-reduce | flops 4 | bytes 32
  21.3 1.3 dynamic_slice.9
  22.6 0.7 pad_add_fusion.info
  23.3 24.0 %all-gather.4.cloned.1.call-done = bf16[2,64,64,128]{3,2,1,0:T(8,128)(2,1)} async-done(((bf16[2,16,64,128]{3,2,1,0:T(8,128)(2,1)}), bf16[2,64,64,128]{3,2,1,0:T(8,128)(2,1)}) %all-gather.4.cloned.1.call-update) | async-done | bytes 2097168 | tf_op jit(solution)/shard_map/all_gather | solution.py:340
  47.2 2.3 dynamic-slice_bitcast_fusion.1.features
  49.5 34.9 %all-gather.6.cloned.1.call-done = bf16[2,64,64,128]{3,2,1,0:T(8,128)(2,1)} async-done(((bf16[2,16,64,128]{3,2,1,0:T(8,128)(2,1)}), bf16[2,64,64,128]{3,2,1,0:T(8,128)(2,1)}) %all-gather.6.cloned.1.call-update) | async-done | bytes 2097168 | tf_op jit(solution)/shard_map/all_gather | solution.py:341
  84.4 2.3 dynamic-slice_bitcast_fusion.cotangent
  86.7 69.3 %all-gather.8.cloned.1.call-done = bf16[4,3,9,128,128]{4,3,2,1,0:T(8,128)(2,1)} async-done(((bf16[1,3,9,128,128]{4,3,2,1,0:T(8,128)(2,1)}), bf16[4,3,9,128,128]{4,3,2,1,0:T(8,128)(2,1)}) %all-gather.8.cloned.1.call-update) | async-done | bytes 3538960 | tf_op jit(solution)/shard_map/all_gather | solution.py:339
  156.0 6.1 %copy.7 = bf16[12,3,3,128,128]{3,4,2,1,0:T(8,128)(2,1)} copy(bf16[12,3,3,128,128]{4,3,2,1,0:T(8,128)(2,1)} %bitcast.13) | data formatting | bytes 7077888 | tf_op jit(solution)/shard_map/reshape | solution.py:342
  162.1 4.4 %rev.3 = bf16[12,3,3,128,128]{3,4,2,1,0:T(8,128)(2,1)} reverse(bf16[12,3,3,128,128]{3,4,2,1,0:T(8,128)(2,1)} %copy.7), dimensions={2} | reverse | bytes 7077888 | tf_op jit(solution)/shard_map/rev | solution.py:344
  166.5 2.0 copy-done.1
  168.5 1.2 copy-done.2
  169.7 1.2 copy-done.3
  171.0 76.3 %chain.1 = bf16[3,9,128,128]{3,2,1,0:T(8,128)(2,1)S(1)} custom-call(s32[3]{0:T(128)S(1)} %pad_add_fusion.info, s32[4]{0:T(128)S(1)} %all-reduce.blocks, bf16[64,64,128]{2,1,0:T(8,128)(2,1)S(1)} %copy-done.2, bf16[64,64,128]{2,1,0:T(8,128)(2,1)S(1)} %copy-done.3, bf16[12,3,384,128]{3,2,1,0:T(8,128)(2,1)S(1)} %bitcast.14, bf16[12,3,384,128]{3,2,1,0:T(8,128)(2,1)S(1)} %bitcast.15), custom_call_target="tpu_custom_call" | custom-call | tf_op jit(solution)/shard_map/chain/pallas_call | solution.py:347
  247.3 0.9 copy-done.4
  248.2 54.2 %all-reduce.3.cloned.1.call-done = bf16[1,3,9,128,128]{4,3,2,1,0:T(8,128)(2,1)} async-done(((bf16[1,3,9,128,128]{4,3,2,1,0:T(8,128)(2,1)}), bf16[1,3,9,128,128]{4,3,2,1,0:T(8,128)(2,1)}) %all-reduce.3.cloned.1.call-update) | async-done | bytes 884752 | tf_op jit(solution)/shard_map/psum | solution.py:361
  302.4 2.6 broadcast_in_dim.7
  (10 shorter events, 0.1 us)
Async XLA Ops:
  6.5 40.7 %all-gather.4.cloned.1.call-start = ((), (), s32[]{:S(2)}) async-start(), calls=%async_computation | async-start | bytes 2621440 | tf_op jit(solution)/shard_map/all_gather | solution.py:340
  7.3 77.2 %all-gather.6.cloned.1.call-start = ((), (), s32[]{:S(2)}) async-start(), calls=%async_computation.1 | async-start | bytes 2621440 | tf_op jit(solution)/shard_map/all_gather | solution.py:341
  8.0 148.0 %all-gather.8.cloned.1.call-start = ((), (), s32[]{:S(2)}) async-start(), calls=%async_computation.2 | async-start | bytes 4423680 | tf_op jit(solution)/shard_map/all_gather | solution.py:339
  8.7 293.6 %all-reduce.3.cloned.1.call-start = ((), (), s32[]{:S(2)}) async-start(), calls=%async_computation.3 | async-start | bytes 1769472 | tf_op jit(solution)/shard_map/psum | solution.py:361
  162.1 4.4 %copy-start = (bf16[4,3,9,128,128]{4,3,2,1,0:T(8,128)(2,1)S(1)}, bf16[4,3,9,128,128]{4,3,2,1,0:T(8,128)(2,1)}, u32[]{:S(2)}) copy-start(bf16[4,3,9,128,128]{4,3,2,1,0:T(8,128)(2,1)} %all-gather.8.cloned.1.call-done) | copy-start | bytes 10616836
  166.5 2.0 copy-start.1
  168.5 1.2 copy-start.2
  169.7 1.2 copy-start.3
  247.3 0.9 copy-start.4
Sparse Core Ops, SparseCore 0:
  9.2 38.0 all-gather.3
  49.1 35.2 all-gather.5
  86.0 69.9 all-gather.7
  248.3 54.0 all-reduce.2
